TPU v7x, 32 devices: a whole 2x2x4 slice. The times are simulated.
32 devices in a mesh: dp: 8 (over z, x), fsdp: 4 (over y, core).
Axes of the slice: x: 2, y: 2, z: 4, core: 2. Of those that a mesh axis runs over, the one named last changes fastest.
Arguments:
- hidden: bfloat16 [512, 64, 768], P(('dp', 'fsdp')), may hold values from -6 to 6
- lengths: int32 [512], P(('dp', 'fsdp')), may hold values from 3 to 64, as said below
- cotangent: bfloat16 [512, 64, 768], P(('dp', 'fsdp')), may hold values from -6 to 6
- attgain: bfloat16 [768], P(('dp', 'fsdp')), may hold values from 0.25 to 1.75
- attshift: bfloat16 [768], P(('dp', 'fsdp')), may hold values from -2 to 2
- querymat: bfloat16 [768, 768], P(None, ('dp', 'fsdp')), may hold values from -0.21875 to 0.21875
- querybias: bfloat16 [768], P(('dp', 'fsdp')), may hold values from -2 to 2
- keymat: bfloat16 [768, 768], P(None, ('dp', 'fsdp')), may hold values from -0.21875 to 0.21875
- valuemat: bfloat16 [768, 768], P(None, ('dp', 'fsdp')), may hold values from -0.21875 to 0.21875
- valuebias: bfloat16 [768], P(('dp', 'fsdp')), may hold values from -2 to 2
- mixmat: bfloat16 [768, 768], P(None, ('dp', 'fsdp')), may hold values from -0.625 to 0.625
- mixbias: bfloat16 [768], P(('dp', 'fsdp')), may hold values from -2 to 2
- mlpgain: bfloat16 [768], P(('dp', 'fsdp')), may hold values from 0.25 to 1.75
- mlpshift: bfloat16 [768], P(('dp', 'fsdp')), may hold values from -2 to 2
- upmat_w: bfloat16 [768, 3072], P(None, ('dp', 'fsdp')), may hold values from -0.21875 to 0.21875
- upbias: bfloat16 [3072], P(('dp', 'fsdp')), may hold values from -2 to 2
- downmat: bfloat16 [3072, 768], P(None, ('dp', 'fsdp')), may hold values from -0.109375 to 0.109375
- downbias: bfloat16 [768], P(('dp', 'fsdp')), may hold values from -2 to 2
Outputs:
- block_out: bfloat16 [512, 64, 768], P(('dp', 'fsdp'))
- input_grad: float32 [512, 64, 768], P(('dp', 'fsdp'))
- attgain_grad: float32 [768], P(('dp', 'fsdp'))
- attshift_grad: float32 [768], P(('dp', 'fsdp'))
- querymat_grad: float32 [768, 768], P(None, ('dp', 'fsdp'))
- querybias_grad: float32 [768], P(('dp', 'fsdp'))
- keymat_grad: float32 [768, 768], P(None, ('dp', 'fsdp'))
- valuemat_grad: float32 [768, 768], P(None, ('dp', 'fsdp'))
- valuebias_grad: float32 [768], P(('dp', 'fsdp'))
- mixmat_grad: float32 [768, 768], P(None, ('dp', 'fsdp'))
- mixbias_grad: float32 [768], P(('dp', 'fsdp'))
- mlpgain_grad: float32 [768], P(('dp', 'fsdp'))
- mlpshift_grad: float32 [768], P(('dp', 'fsdp'))
- upmat_grad: float32 [768, 3072], P(None, ('dp', 'fsdp'))
- upbias_grad: float32 [3072], P(('dp', 'fsdp'))
- downmat_grad: float32 [3072, 768], P(None, ('dp', 'fsdp'))
- downbias_grad: float32 [768], P(('dp', 'fsdp'))
Inputs may be any that keep to these rules, and one draw needn't show every extreme that they name: The first lengths[c] token slots of caption c are real, the rest padding; some caption has 64 real tokens and some has 3.
All inputs are finite; a program needn't handle non-finite values.
Results may differ from a plain program's by a relative error of at most 0.013.
Values may be sent and summed in bfloat16 or wider, within the bound.
No kernel may reach another device: no remote copies, remote signals or barrier semaphores. Data moves between devices by JAX's collectives and lax.ppermute only.
A program may use at most 192 MiB of HBM per device.

v0:
```python
import math
import jax
import jax.numpy as jnp
from jax import lax
from jax.sharding import PartitionSpec as P

HEADS = 12


def layer_norm(values, gain, shift):
    centre = jnp.mean(values, axis=-1, keepdims=True)
    centred = values - centre
    spread = jnp.mean(centred * centred, axis=-1, keepdims=True)
    return centred * lax.rsqrt(spread + 1e-06) * gain + shift


def smooth(values):
    return jax.nn.gelu(values, approximate=True)


def project(inputs, matrix):
    return jnp.einsum("cli,ij->clj", inputs, matrix, preferred_element_type=jnp.float32)


def project_back(grads, matrix):
    return jnp.einsum("clj,ij->cli", grads, matrix, preferred_element_type=jnp.float32)


def outer_sum(inputs, grads):
    return jnp.einsum("cli,clj->ij", inputs, grads, preferred_element_type=jnp.float32)


def token_sum(grads):
    return jnp.sum(grads.astype(jnp.float32), axis=(0, 1))


def masked_scores(query_low, keys_low, keymask, factor):
    raw = (
        jnp.einsum("clhd,cmhd->chlm", query_low, keys_low, preferred_element_type=jnp.float32)
        * factor
    )
    return jnp.where(keymask[:, None, None, :], raw, -1e30)


def per_device(
    hidden,
    lengths,
    cotangent,
    attgain,
    attshift,
    querymat,
    querybias,
    keymat,
    valuemat,
    valuebias,
    mixmat,
    mixbias,
    mlpgain,
    mlpshift,
    upmat_w,
    upbias,
    downmat,
    downbias,
):
    captions, length, width = hidden.shape
    head_size = width // HEADS
    factor = 1.0 / math.sqrt(head_size)
    positions = lax.broadcasted_iota(jnp.int32, (captions, length), 1)
    keymask = positions < lengths[:, None]
    rowmask = keymask.astype(jnp.float32)[..., None]
    gathered = (
        lax.all_gather(attgain, ("dp", "fsdp"), axis=0, tiled=True),
        lax.all_gather(attshift, ("dp", "fsdp"), axis=0, tiled=True),
        lax.all_gather(querymat, ("dp", "fsdp"), axis=1, tiled=True),
        lax.all_gather(querybias, ("dp", "fsdp"), axis=0, tiled=True),
        lax.all_gather(keymat, ("dp", "fsdp"), axis=1, tiled=True),
        lax.all_gather(valuemat, ("dp", "fsdp"), axis=1, tiled=True),
        lax.all_gather(valuebias, ("dp", "fsdp"), axis=0, tiled=True),
        lax.all_gather(mixmat, ("dp", "fsdp"), axis=1, tiled=True),
        lax.all_gather(mixbias, ("dp", "fsdp"), axis=0, tiled=True),
        lax.all_gather(mlpgain, ("dp", "fsdp"), axis=0, tiled=True),
        lax.all_gather(mlpshift, ("dp", "fsdp"), axis=0, tiled=True),
        lax.all_gather(upmat_w, ("dp", "fsdp"), axis=1, tiled=True),
        lax.all_gather(upbias, ("dp", "fsdp"), axis=0, tiled=True),
        lax.all_gather(downmat, ("dp", "fsdp"), axis=1, tiled=True),
        lax.all_gather(downbias, ("dp", "fsdp"), axis=0, tiled=True),
    )
    (
        gain_one,
        shift_one,
        query_w,
        query_b,
        keys_w,
        values_w,
        values_b,
        mixer_w,
        mixer_b,
        gain_two,
        shift_two,
        upper_w,
        upper_b,
        lower_w,
        lower_b,
    ) = gathered
    gain_one = gain_one.astype(jnp.float32)
    shift_one = shift_one.astype(jnp.float32)
    gain_two = gain_two.astype(jnp.float32)
    shift_two = shift_two.astype(jnp.float32)
    source = hidden.astype(jnp.float32)
    normed_low = layer_norm(source, gain_one, shift_one).astype(jnp.bfloat16)
    query_low = (project(normed_low, query_w) + query_b.astype(jnp.float32)).astype(jnp.bfloat16)
    keys_low = project(normed_low, keys_w).astype(jnp.bfloat16)
    values_low = (project(normed_low, values_w) + values_b.astype(jnp.float32)).astype(jnp.bfloat16)
    query_heads = query_low.reshape(captions, length, HEADS, head_size)
    keys_heads = keys_low.reshape(captions, length, HEADS, head_size)
    values_heads = values_low.reshape(captions, length, HEADS, head_size)
    scores = masked_scores(query_heads, keys_heads, keymask, factor)
    peak = jnp.max(scores, axis=-1, keepdims=True)
    logsum = peak + jnp.log(jnp.sum(jnp.exp(scores - peak), axis=-1, keepdims=True))
    probs_low = jnp.exp(scores - logsum).astype(jnp.bfloat16)
    mixed_low = (
        jnp.einsum("chlm,cmhd->clhd", probs_low, values_heads, preferred_element_type=jnp.float32)
        .reshape(captions, length, width)
        .astype(jnp.bfloat16)
    )
    middle = source + project(mixed_low, mixer_w) + mixer_b.astype(jnp.float32)
    normed2_low = layer_norm(middle, gain_two, shift_two).astype(jnp.bfloat16)
    upper = project(normed2_low, upper_w) + upper_b.astype(jnp.float32)
    active_low = smooth(upper).astype(jnp.bfloat16)
    result = middle + project(active_low, lower_w) + lower_b.astype(jnp.float32)
    block_out = result.astype(jnp.bfloat16)
    again = (
        lax.all_gather(attgain, ("dp", "fsdp"), axis=0, tiled=True),
        lax.all_gather(attshift, ("dp", "fsdp"), axis=0, tiled=True),
        lax.all_gather(querymat, ("dp", "fsdp"), axis=1, tiled=True),
        lax.all_gather(querybias, ("dp", "fsdp"), axis=0, tiled=True),
        lax.all_gather(keymat, ("dp", "fsdp"), axis=1, tiled=True),
        lax.all_gather(valuemat, ("dp", "fsdp"), axis=1, tiled=True),
        lax.all_gather(valuebias, ("dp", "fsdp"), axis=0, tiled=True),
        lax.all_gather(mixmat, ("dp", "fsdp"), axis=1, tiled=True),
        lax.all_gather(mixbias, ("dp", "fsdp"), axis=0, tiled=True),
        lax.all_gather(mlpgain, ("dp", "fsdp"), axis=0, tiled=True),
        lax.all_gather(mlpshift, ("dp", "fsdp"), axis=0, tiled=True),
        lax.all_gather(upmat_w, ("dp", "fsdp"), axis=1, tiled=True),
        lax.all_gather(upbias, ("dp", "fsdp"), axis=0, tiled=True),
        lax.all_gather(downmat, ("dp", "fsdp"), axis=1, tiled=True),
        lax.all_gather(downbias, ("dp", "fsdp"), axis=0, tiled=True),
    )
    (
        gain_one,
        shift_one,
        query_w,
        query_b,
        keys_w,
        values_w,
        values_b,
        mixer_w,
        mixer_b,
        gain_two,
        shift_two,
        upper_w,
        upper_b,
        lower_w,
        lower_b,
    ) = again
    gain_one = gain_one.astype(jnp.float32)
    shift_one = shift_one.astype(jnp.float32)
    gain_two = gain_two.astype(jnp.float32)
    shift_two = shift_two.astype(jnp.float32)
    grad_out = cotangent.astype(jnp.float32) * rowmask
    grad_low = grad_out.astype(jnp.bfloat16)
    downmat_grad = outer_sum(active_low, grad_low)
    downbias_grad = token_sum(grad_low)
    grad_active = project_back(grad_low, lower_w)
    gelu_pull = jax.vjp(smooth, upper)[1]
    grad_upper_low = gelu_pull(grad_active)[0].astype(jnp.bfloat16)
    upmat_grad = outer_sum(normed2_low, grad_upper_low)
    upbias_grad = token_sum(grad_upper_low)
    grad_normed2 = project_back(grad_upper_low, upper_w)
    norm_pull = jax.vjp(layer_norm, middle, gain_two, shift_two)[1]
    grad_ln_two, mlpgain_grad, mlpshift_grad = norm_pull(grad_normed2)
    grad_middle = grad_out + grad_ln_two
    mlpgain_grad, mlpshift_grad, upmat_grad, upbias_grad, downmat_grad, downbias_grad = (
        lax.psum_scatter(mlpgain_grad, ("dp", "fsdp"), scatter_dimension=0, tiled=True),
        lax.psum_scatter(mlpshift_grad, ("dp", "fsdp"), scatter_dimension=0, tiled=True),
        lax.psum_scatter(upmat_grad, ("dp", "fsdp"), scatter_dimension=1, tiled=True),
        lax.psum_scatter(upbias_grad, ("dp", "fsdp"), scatter_dimension=0, tiled=True),
        lax.psum_scatter(downmat_grad, ("dp", "fsdp"), scatter_dimension=1, tiled=True),
        lax.psum_scatter(downbias_grad, ("dp", "fsdp"), scatter_dimension=0, tiled=True),
    )
    grad_branch_low = grad_middle.astype(jnp.bfloat16)
    mixmat_grad = outer_sum(mixed_low, grad_branch_low)
    mixbias_grad = token_sum(grad_branch_low)
    grad_mixed_low = (
        project_back(grad_branch_low, mixer_w)
        .astype(jnp.bfloat16)
        .reshape(captions, length, HEADS, head_size)
    )
    scores_again = masked_scores(query_heads, keys_heads, keymask, factor)
    probs = jnp.exp(scores_again - logsum)
    probs_again = probs.astype(jnp.bfloat16)
    grad_values_low = jnp.einsum(
        "chlm,clhd->cmhd", probs_again, grad_mixed_low, preferred_element_type=jnp.float32
    ).astype(jnp.bfloat16)
    grad_probs = jnp.einsum(
        "clhd,cmhd->chlm", grad_mixed_low, values_heads, preferred_element_type=jnp.float32
    )
    weighted = jnp.sum(probs * grad_probs, axis=-1, keepdims=True)
    grad_scores_low = (probs * (grad_probs - weighted)).astype(jnp.bfloat16)
    grad_query_low = (
        jnp.einsum(
            "chlm,cmhd->clhd", grad_scores_low, keys_heads, preferred_element_type=jnp.float32
        )
        * factor
    ).astype(jnp.bfloat16)
    grad_keys_low = (
        jnp.einsum(
            "chlm,clhd->cmhd", grad_scores_low, query_heads, preferred_element_type=jnp.float32
        )
        * factor
    ).astype(jnp.bfloat16)
    grad_query_low = grad_query_low.reshape(captions, length, width)
    grad_keys_low = grad_keys_low.reshape(captions, length, width)
    grad_values_low = grad_values_low.reshape(captions, length, width)
    querymat_grad = outer_sum(normed_low, grad_query_low)
    querybias_grad = token_sum(grad_query_low)
    keymat_grad = outer_sum(normed_low, grad_keys_low)
    valuemat_grad = outer_sum(normed_low, grad_values_low)
    valuebias_grad = token_sum(grad_values_low)
    grad_normed = (
        project_back(grad_query_low, query_w)
        + project_back(grad_keys_low, keys_w)
        + project_back(grad_values_low, values_w)
    )
    first_pull = jax.vjp(layer_norm, source, gain_one, shift_one)[1]
    grad_ln_one, attgain_grad, attshift_grad = first_pull(grad_normed)
    input_grad = grad_middle + grad_ln_one
    (
        attgain_grad,
        attshift_grad,
        querymat_grad,
        querybias_grad,
        keymat_grad,
        valuemat_grad,
        valuebias_grad,
        mixmat_grad,
        mixbias_grad,
    ) = (
        lax.psum_scatter(attgain_grad, ("dp", "fsdp"), scatter_dimension=0, tiled=True),
        lax.psum_scatter(attshift_grad, ("dp", "fsdp"), scatter_dimension=0, tiled=True),
        lax.psum_scatter(querymat_grad, ("dp", "fsdp"), scatter_dimension=1, tiled=True),
        lax.psum_scatter(querybias_grad, ("dp", "fsdp"), scatter_dimension=0, tiled=True),
        lax.psum_scatter(keymat_grad, ("dp", "fsdp"), scatter_dimension=1, tiled=True),
        lax.psum_scatter(valuemat_grad, ("dp", "fsdp"), scatter_dimension=1, tiled=True),
        lax.psum_scatter(valuebias_grad, ("dp", "fsdp"), scatter_dimension=0, tiled=True),
        lax.psum_scatter(mixmat_grad, ("dp", "fsdp"), scatter_dimension=1, tiled=True),
        lax.psum_scatter(mixbias_grad, ("dp", "fsdp"), scatter_dimension=0, tiled=True),
    )
    return (
        block_out,
        input_grad,
        attgain_grad,
        attshift_grad,
        querymat_grad,
        querybias_grad,
        keymat_grad,
        valuemat_grad,
        valuebias_grad,
        mixmat_grad,
        mixbias_grad,
        mlpgain_grad,
        mlpshift_grad,
        upmat_grad,
        upbias_grad,
        downmat_grad,
        downbias_grad,
    )


def solution(mesh):
    placed = (
        P(("dp", "fsdp"), None, None),
        P(("dp", "fsdp")),
        P(("dp", "fsdp"), None, None),
        P(("dp", "fsdp")),
        P(("dp", "fsdp")),
        P(None, ("dp", "fsdp")),
        P(("dp", "fsdp")),
        P(None, ("dp", "fsdp")),
        P(None, ("dp", "fsdp")),
        P(("dp", "fsdp")),
        P(None, ("dp", "fsdp")),
        P(("dp", "fsdp")),
        P(("dp", "fsdp")),
        P(("dp", "fsdp")),
        P(None, ("dp", "fsdp")),
        P(("dp", "fsdp")),
        P(None, ("dp", "fsdp")),
        P(("dp", "fsdp")),
    )
    return jax.shard_map(
        per_device,
        mesh=mesh,
        in_specs=placed,
        out_specs=(
            P(("dp", "fsdp"), None, None),
            P(("dp", "fsdp"), None, None),
            P(("dp", "fsdp")),
            P(("dp", "fsdp")),
            P(None, ("dp", "fsdp")),
            P(("dp", "fsdp")),
            P(None, ("dp", "fsdp")),
            P(None, ("dp", "fsdp")),
            P(("dp", "fsdp")),
            P(None, ("dp", "fsdp")),
            P(("dp", "fsdp")),
            P(("dp", "fsdp")),
            P(("dp", "fsdp")),
            P(None, ("dp", "fsdp")),
            P(("dp", "fsdp")),
            P(None, ("dp", "fsdp")),
            P(("dp", "fsdp")),
        ),
        check_vma=False,
    )
```

profile of v0, /device:TPU:0, one launch (start us, length us, event | category | flops | bytes accessed | tf_op | source)
XLA Modules:
  0.0 1099.5 jit_solution(7005276852524164736)
XLA Ops:
  18.8 42.7 %all-reduce.19 = (bf16[768]{0:T(1024)(128)(2,1)S(1)}, bf16[768]{0:T(1024)(128)(2,1)S(1)}, bf16[768]{0:T(1024)(128)(2,1)S(1)}, bf16[768]{0:T(1024)(128)(2,1)S(1)}...) all-reduce(bf16[768]{0:T(1024)(128)(2,1)S(1)} %dynamic-update-slice, ...), channel_id=1, replica_groups=mesh['dp'=8,'fsdp'=4] {'dp','fsdp'}, use_global_device_ids=true, to_apply=%add.2 | all-reduce | flops 9216 | bytes 36864
  65.1 2.8 all-gather.9.cloned.1.call-done
  68.0 2.9 add_convert_fusion.2
  70.9 2.7 copy.89
  73.6 50.5 %all-gather.11.cloned.1.call-done = bf16[768,768]{0,1:T(8,128)(2,1)} async-done(((bf16[768,24]{0,1:T(8,128)(2,1)}), bf16[768,768]{0,1:T(8,128)(2,1)}) %all-gather.11.cloned.1.call-update) | async-done | bytes 1179664 | tf_op jit(solution)/shard_map/all_gather | solution.py:76
  124.1 2.9 convolution_convert_fusion.2
  127.0 3.9 reshape.173
  130.9 49.2 %all-gather.7.cloned.1.call-done = bf16[768,768]{0,1:T(8,128)(2,1)} async-done(((bf16[768,24]{0,1:T(8,128)(2,1)}), bf16[768,768]{0,1:T(8,128)(2,1)}) %all-gather.7.cloned.1.call-update) | async-done | bytes 1179664 | tf_op jit(solution)/shard_map/all_gather | solution.py:77
  180.1 2.9 add_convert_fusion.3
  183.0 3.9 reshape.171
  186.9 4.8 fusion.7
  191.7 1.8 exponential_reduce_fusion
  196.1 4.0 convolution_convert_fusion
  200.1 35.8 %all-gather.13.cloned.1.call-done = bf16[768,768]{0,1:T(8,128)(2,1)} async-done(((bf16[768,24]{0,1:T(8,128)(2,1)}), bf16[768,768]{0,1:T(8,128)(2,1)}) %all-gather.13.cloned.1.call-update) | async-done | bytes 1179664 | tf_op jit(solution)/shard_map/all_gather | solution.py:79
  235.9 5.0 fusion.76
  243.0 58.2 %all-gather.15.cloned.1.call-done = bf16[768,3072]{0,1:T(8,128)(2,1)} async-done(((bf16[768,96]{0,1:T(8,128)(2,1)}), bf16[768,3072]{0,1:T(8,128)(2,1)}) %all-gather.15.cloned.1.call-update) | async-done | bytes 4718608 | tf_op jit(solution)/shard_map/all_gather | solution.py:83
  301.2 11.0 fusion.18
  312.2 54.2 %all-gather.17.cloned.1.call-done = bf16[3072,768]{0,1:T(8,128)(2,1)} async-done(((bf16[3072,24]{0,1:T(8,128)(2,1)}), bf16[3072,768]{0,1:T(8,128)(2,1)}) %all-gather.17.cloned.1.call-update) | async-done | bytes 4718608 | tf_op jit(solution)/shard_map/all_gather | solution.py:85
  366.4 16.4 %convert_reduce_fusion = (f32[3072]{0:T(1024)S(1)}, bf16[16,64,3072]{2,1,0:T(8,128)(2,1)S(1)}) fusion(f32[16,64,3072]{2,1,0:T(8,128)} %fusion.18, f32[3072]{0:T(1024)S(1)} %convert_element_type.143, bf16[3072,768]{0,1:T(8,128)(2,1)} %all-gather.17.cloned.1.call-done, bf16[16,64,768]{2,1,0:T(8,128)(2,1)S(1)} %copy-done.11, f32[16,64]{1,0:T(8,128)S(1)} %get-tuple-element.47), kind=kOutput, calls=%fused_computation.9 | convolution fusion | flops 4906546176 | bytes 25194496 | tf_op jit(solution)/shard_map/clj,ij->cli/dot_general | solution.py:26
  382.8 5.5 multiply_reduce_fusion.1
  393.3 4.1 convolution_bitcast_fusion.2
  397.4 4.0 convolution_convert_fusion.1
  401.4 6.2 reshape.174
  407.6 9.3 multiply_reduce_fusion
  416.9 2.6 multiply_convert_fusion.3
  421.3 4.7 copy.79
  425.9 6.2 reshape.176
  432.2 4.7 convolution_bitcast_fusion.4
  437.3 5.0 convert_reduce_fusion.2
  442.3 4.6 copy.75
  447.0 6.1 reshape.175
  453.1 4.7 convolution_bitcast_fusion.5
  458.0 6.6 convert_reduce_fusion.1
  464.5 4.6 copy.81
  469.2 5.2 reshape.177
  474.4 3.2 convolution_bitcast_fusion.3
  477.7 11.0 %convolution_bitcast_fusion.1 = f32[768,3072]{0,1:T(8,128)} fusion(bf16[16,64,3072]{2,1,0:T(8,128)(2,1)} %copy-done.23, f32[16,64,768]{2,1,0:T(8,128)} %copy-done.7, f32[768]{0:T(1024)S(1)} %convert_element_type.141, f32[768]{0:T(1024)S(1)} %convert_element_type.140, f32[16,64]{1,0:T(8,128)S(1)} %fusion.61, f32[16,64]{1,0:T(8,128)S(1)} %broadcast_multiply_fusion), kind=kOutput, calls=%fused_computation.21 | convolution fusion | flops 4835770368 | bytes 18888704 | tf_op jit(solution)/shard_map/cli,clj->ij/dot_general | solution.py:30
  489.0 12.2 %convolution_bitcast_fusion = f32[3072,768]{0,1:T(8,128)} fusion(bf16[16,64,768]{2,1,0:T(8,128)(2,1)} %param.20, f32[16,64]{1,0:T(8,128)S(1)} %get-tuple-element.47, f32[16,64,3072]{2,1,0:T(8,128)} %fusion.18, f32[3072]{0:T(1024)S(1)} %convert_element_type.143), kind=kOutput, calls=%fused_computation.20 | convolution fusion | flops 4865654784 | bytes 23609344 | tf_op jit(solution)/shard_map/cli,clj->ij/dot_general | solution.py:30
  502.0 3.3 fusion.50
  506.7 1.9 fusion.73
  512.0 40.8 %all-reduce.18 = (f32[768]{0:T(1024)S(1)}, f32[768]{0:T(1024)S(1)}, f32[768]{0:T(1024)S(1)}, f32[768]{0:T(1024)S(1)}, f32[768]{0:T(1024)S(1)}, /*index=5*/f32[76...) all-reduce(f32[768]{0:T(1024)S(1)} %get-tuple-element.19, ...), channel_id=2, replica_groups=mesh['dp'=8,'fsdp'=4] {'dp','fsdp'}, use_global_device_ids=true, to_apply=%region_12.13.clone | all-reduce | flops 9216 | bytes 73728
  558.1 5.0 add_add_fusion.2
  563.1 13.2 %add_convert_fusion = bf16[16,64,768]{2,1,0:T(8,128)(2,1)} fusion(f32[16,64,768]{2,1,0:T(8,128)S(1)} %copy-done.9, bf16[3072,768]{0,1:T(8,128)(2,1)} %all-gather.17.cloned.1.call-done, f32[768]{0:T(1024)S(1)} %convert_element_type.145, f32[16,64,3072]{2,1,0:T(8,128)} %fusion.18, f32[3072]{0:T(1024)S(1)} %convert_element_type.143), kind=kOutput, calls=%fused_computation.61 | convolution fusion | flops 4865654784 | bytes 22035456 | tf_op jit(solution)/shard_map/cli,ij->clj/dot_general | solution.py:22
  576.3 24.0 %reduce-scatter.9.cloned.1.call-done = f32[768,24]{0,1:T(8,128)} async-done(((f32[768,768]{0,1:T(8,128)}), f32[768,24]{0,1:T(8,128)}) %reduce-scatter.9.cloned.1.call-update) | async-done | bytes 73744 | tf_op jit(solution)/shard_map/reduce_scatter | solution.py:253
  600.4 103.9 %reduce-scatter.7.cloned.1.call-done = f32[768,24]{0,1:T(8,128)} async-done(((f32[768,768]{0,1:T(8,128)}), f32[768,24]{0,1:T(8,128)}) %reduce-scatter.7.cloned.1.call-update) | async-done | bytes 73744 | tf_op jit(solution)/shard_map/reduce_scatter | solution.py:251
  704.3 104.7 %reduce-scatter.11.cloned.1.call-done = f32[768,24]{0,1:T(8,128)} async-done(((f32[768,768]{0,1:T(8,128)}), f32[768,24]{0,1:T(8,128)}) %reduce-scatter.11.cloned.1.call-update) | async-done | bytes 73744 | tf_op jit(solution)/shard_map/reduce_scatter | solution.py:254
  809.0 141.2 %reduce-scatter.15.cloned.1.call-done = f32[768,96]{0,1:T(8,128)} async-done(((f32[768,3072]{0,1:T(8,128)}), f32[768,96]{0,1:T(8,128)}) %reduce-scatter.15.cloned.1.call-update) | async-done | bytes 294928 | tf_op jit(solution)/shard_map/reduce_scatter | solution.py:186
  950.2 142.0 %reduce-scatter.17.cloned.1.call-done = f32[3072,24]{0,1:T(8,128)} async-done(((f32[3072,768]{0,1:T(8,128)}), f32[3072,24]{0,1:T(8,128)}) %reduce-scatter.17.cloned.1.call-update) | async-done | bytes 294928 | tf_op jit(solution)/shard_map/reduce_scatter | solution.py:188
  (134 shorter events, 38.3 us)
Async XLA Ops:
  7.2 56.8 %copy-start.1 = (bf16[16,64,768]{2,1,0:T(8,128)(2,1)S(1)}, bf16[16,64,768]{2,1,0:T(8,128)(2,1)}, u32[]{:S(2)}) copy-start(bf16[16,64,768]{2,1,0:T(8,128)(2,1)} %param.18) | copy-start | bytes 4718596
  7.2 60.8 %all-gather.9.cloned.1.call-start = ((), (), s32[]{:S(2)}) async-start(), calls=%async_computation.7 | async-start | bytes 1216512 | tf_op jit(solution)/shard_map/all_gather | solution.py:74
  7.9 116.2 %all-gather.11.cloned.1.call-start = ((), (), s32[]{:S(2)}) async-start(), calls=%async_computation.8 | async-start | bytes 1216512 | tf_op jit(solution)/shard_map/all_gather | solution.py:76
  8.7 171.4 %all-gather.7.cloned.1.call-start = ((), (), s32[]{:S(2)}) async-start(), calls=%async_computation.6 | async-start | bytes 1216512 | tf_op jit(solution)/shard_map/all_gather | solution.py:77
  9.4 226.5 %all-gather.13.cloned.1.call-start = ((), (), s32[]{:S(2)}) async-start(), calls=%async_computation.9 | async-start | bytes 1216512 | tf_op jit(solution)/shard_map/all_gather | solution.py:79
  10.0 291.2 %all-gather.15.cloned.1.call-start = ((), (), s32[]{:S(2)}) async-start(), calls=%async_computation.10 | async-start | bytes 4866048 | tf_op jit(solution)/shard_map/all_gather | solution.py:83
  10.6 355.8 %all-gather.17.cloned.1.call-start = ((), (), s32[]{:S(2)}) async-start(), calls=%async_computation.11 | async-start | bytes 4866048 | tf_op jit(solution)/shard_map/all_gather | solution.py:85
  11.2 565.2 %reduce-scatter.13.cloned.1.call-start = ((), (), s32[]{:S(2)}) async-start(), calls=%async_computation.15 | async-start | bytes 2433024 | tf_op jit(solution)/shard_map/reduce_scatter | solution.py:256
  64.5 0.6 copy-start.17
  191.6 3.2 copy-start
  191.7 4.5 copy-start.6
  240.9 1.6 copy-start.7
  243.0 123.4 %copy-start.11 = (bf16[16,64,768]{2,1,0:T(8,128)(2,1)S(1)}, bf16[16,64,768]{2,1,0:T(8,128)(2,1)}, u32[]{:S(2)}) copy-start(bf16[16,64,768]{2,1,0:T(8,128)(2,1)} %param.20) | copy-start | bytes 4718596
  366.4 16.4 %copy-start.8 = (f32[16,64,768]{2,1,0:T(8,128)S(1)}, f32[16,64,768]{2,1,0:T(8,128)}, u32[]{:S(2)}) copy-start(f32[16,64,768]{2,1,0:T(8,128)} %copy-done.7) | copy-start | bytes 9437188
  366.4 16.4 %copy-start.20 = (bf16[768,3072]{0,1:T(8,128)(2,1)S(1)}, bf16[768,3072]{0,1:T(8,128)(2,1)}, u32[]{:S(2)}) copy-start(bf16[768,3072]{0,1:T(8,128)(2,1)} %all-gather.15.cloned.1.call-done) | copy-start | bytes 14155780
  382.8 5.6 copy-start.23
  389.7 1.7 copy-start.3
  389.7 3.6 copy-start.13
  391.4 1.1 copy-start.15
  393.3 4.1 copy-start.22
  397.3 203.0 %reduce-scatter.9.cloned.1.call-start = ((), (), s32[]{:S(2)}) async-start(), calls=%async_computation.13 | async-start | bytes 2433024 | tf_op jit(solution)/shard_map/reduce_scatter | solution.py:253
  401.4 15.5 %slice-start = ((s8[6291456]{0:T(1024)(128)(4,1)}), s8[2097152]{0:T(1024)(128)(4,1)S(1)}, s32[]{:S(2)}) async-start(s8[6291456]{0:T(1024)(128)(4,1)} %bitcast.80), calls=%async_computation.18 | async-start | bytes 4194304
  407.6 9.3 slice-start.1
  416.9 2.6 copy-start.4
  419.5 1.8 copy-start.10
  425.9 6.2 copy-start.2
  436.9 267.4 %reduce-scatter.7.cloned.1.call-start = ((), (), s32[]{:S(2)}) async-start(), calls=%async_computation.12 | async-start | bytes 2433024 | tf_op jit(solution)/shard_map/reduce_scatter | solution.py:251
  457.8 351.2 %reduce-scatter.11.cloned.1.call-start = ((), (), s32[]{:S(2)}) async-start(), calls=%async_computation.14 | async-start | bytes 2433024 | tf_op jit(solution)/shard_map/reduce_scatter | solution.py:254
  477.6 472.6 %reduce-scatter.15.cloned.1.call-start = ((), (), s32[]{:S(2)}) async-start(), calls=%async_computation.16 | async-start | bytes 9732096 | tf_op jit(solution)/shard_map/reduce_scatter | solution.py:186
  488.7 603.5 %reduce-scatter.17.cloned.1.call-start = ((), (), s32[]{:S(2)}) async-start(), calls=%async_computation.17 | async-start | bytes 9732096 | tf_op jit(solution)/shard_map/reduce_scatter | solution.py:188
  501.2 0.7 copy-start.19
  502.0 3.3 copy-start.14
  502.0 3.3 copy-start.21
  505.3 1.4 copy-start.16
  506.7 2.0 copy-start.18
  508.7 1.7 copy-start.5
  508.7 49.4 %copy-start.12 = (bf16[16,64,768]{2,1,0:T(8,128)(2,1)S(1)}, bf16[16,64,768]{2,1,0:T(8,128)(2,1)}, u32[]{:S(2)}) copy-start(bf16[16,64,768]{2,1,0:T(8,128)(2,1)} %param.20) | copy-start | bytes 4718596
  558.1 5.0 copy-start.9
Sparse Core Ops, SparseCore 0:
  10.9 56.9 all-gather.8
  70.9 53.1 all-gather.10
  127.0 53.0 all-gather.6
  182.8 53.0 all-gather.12
  238.6 62.5 all-gather.14
  304.0 62.3 all-gather.16
  397.5 97.8 reduce-scatter.12
  502.1 98.2 reduce-scatter.8
  606.2 98.0 reduce-scatter.6
  710.8 98.0 reduce-scatter.10
  815.5 134.6 reduce-scatter.14
  957.5 134.6 reduce-scatter.16
where the time goes:
time: 1110 us; the launch traced here: 1100 us
  waiting for transfers between devices  770 us (69%)
  matrix products  142 us (13%)
  blocking collectives  83.5 us (8%)
  local copies, waits for them, and re-layouts  71 us (6%)
  other arithmetic  16.6 us (1%)
  between operations  15.2 us (1%)
    reduce_scatter x1, waiting for transfers between devices, per_device(): lax.psum_scatter(downmat_grad, ('dp', 'fsdp'), scatter_dimension=1, tiled...  142 us
    reduce_scatter x1, waiting for transfers between devices, per_device(): lax.psum_scatter(upmat_grad, ('dp', 'fsdp'), scatter_dimension=1, tiled=T...  141 us
    reduce_scatter x1, waiting for transfers between devices, per_device(): lax.psum_scatter(valuemat_grad, ('dp', 'fsdp'), scatter_dimension=1, tile...  105 us
    reduce_scatter x1, waiting for transfers between devices, per_device(): lax.psum_scatter(querymat_grad, ('dp', 'fsdp'), scatter_dimension=1, tile...  104 us
    unnamed x2, blocking collectives  83.5 us
    all_gather x1, waiting for transfers between devices, per_device(): lax.all_gather(upmat_w, ('dp', 'fsdp'), axis=1, tiled=True)  58.2 us
    all_gather x1, waiting for transfers between devices, per_device(): lax.all_gather(downmat, ('dp', 'fsdp'), axis=1, tiled=True)  54.2 us
    all_gather x1, waiting for transfers between devices, per_device(): lax.all_gather(keymat, ('dp', 'fsdp'), axis=1, tiled=True)  50.5 us
  transfers between devices with their start and end apart: 12, of which 11 were waited for; matrix products, arithmetic and copies ran while one was open for 17% of the time, Pallas kernels for 0%

commit v1 on v0

--- a/solution.py
+++ b/solution.py
@@ -1,3 +1,4 @@
+import functools
 import math
 import jax
 import jax.numpy as jnp
@@ -5,6 +6,23 @@
 from jax.sharding import PartitionSpec as P
 
 HEADS = 12
+
+
+def _update_object(point, named_axis):
+    prior, arr_out = (jax.lax.axis_size(named_axis), jax.lax.axis_index(named_axis))
+    v_now, right_arr = (point, 1)
+    while right_arr < prior:
+        n_now = jax.lax.ppermute(
+            v_now, named_axis, perm=[(tick, tick ^ right_arr) for tick in range(prior)]
+        )
+        a_next = jnp.concatenate([v_now, n_now], axis=1)
+        reached = jnp.concatenate([n_now, v_now], axis=1)
+        v_now = jnp.where(arr_out & right_arr == 0, a_next, reached)
+        right_arr = 2 * right_arr
+    return v_now
+
+
+finish_the_rounds = functools.partial(_update_object, named_axis=("dp", "fsdp"))
 
 
 def layer_norm(values, gain, shift):
@@ -82,7 +100,7 @@
         lax.all_gather(mlpshift, ("dp", "fsdp"), axis=0, tiled=True),
         lax.all_gather(upmat_w, ("dp", "fsdp"), axis=1, tiled=True),
         lax.all_gather(upbias, ("dp", "fsdp"), axis=0, tiled=True),
-        lax.all_gather(downmat, ("dp", "fsdp"), axis=1, tiled=True),
+        finish_the_rounds(downmat),
         lax.all_gather(downbias, ("dp", "fsdp"), axis=0, tiled=True),
     )
     (

time: 1110 us -> 1220 us (1.099)
  blocking collectives: 83.5 us -> 156 us
  waiting for transfers between devices: 770 us -> 786 us
    reduce_scatter x1, waiting for transfers between devices: 104 us -> 0.01 us  [per_device(): lax.psum_scatter(querymat_grad, ('dp', 'fsdp'), scatter_dimension=1, tile...]
    reduce_scatter x1, waiting for transfers between devices: 0.01 us -> 96.6 us  [per_device(): lax.psum_scatter(mixmat_grad, ('dp', 'fsdp'), scatter_dimension=1, tiled=...]
    unnamed x2, blocking collectives: 83.5 us -> 156 us
    ppermute x0 -> x5, waiting for transfers between devices: none -> 47.5 us  [_update_object(): jax.lax.ppermute(v_now, named_axis, perm=[(tick, tick ^ right_arr) for ti...]
    reduce_scatter x1, waiting for transfers between devices: 24 us -> 0.01 us  [per_device(): lax.psum_scatter(keymat_grad, ('dp', 'fsdp'), scatter_dimension=1, tiled=...]
  transfers between devices with their start and end apart: 12 -> 17, of which waited for: 11 -> 14; matrix products, arithmetic and copies ran while one was open for 17% -> 14% of each run, Pallas kernels for 0% -> 0%
where the time goes in v1:
time: 1220 us; the launch traced here: 1210 us
  waiting for transfers between devices  786 us (64%)
  blocking collectives  156 us (13%)
  matrix products  147 us (12%)
  local copies, waits for them, and re-layouts  70.7 us (6%)
  other arithmetic  26.9 us (2%)
  between operations  15.1 us (1%)
    unnamed x2, blocking collectives  156 us
    reduce_scatter x1, waiting for transfers between devices, per_device(): lax.psum_scatter(downmat_grad, ('dp', 'fsdp'), scatter_dimension=1, tiled...  142 us
    reduce_scatter x1, waiting for transfers between devices, per_device(): lax.psum_scatter(upmat_grad, ('dp', 'fsdp'), scatter_dimension=1, tiled=T...  141 us
    reduce_scatter x1, waiting for transfers between devices, per_device(): lax.psum_scatter(valuemat_grad, ('dp', 'fsdp'), scatter_dimension=1, tile...  105 us
    reduce_scatter x1, waiting for transfers between devices, per_device(): lax.psum_scatter(mixmat_grad, ('dp', 'fsdp'), scatter_dimension=1, tiled=...  96.6 us
    all_gather x1, waiting for transfers between devices, per_device(): lax.all_gather(upmat_w, ('dp', 'fsdp'), axis=1, tiled=True)  58.2 us
    all_gather x1, waiting for transfers between devices, per_device(): lax.all_gather(downmat, ('dp', 'fsdp'), axis=1, tiled=True)  54.3 us
    all_gather x1, waiting for transfers between devices, per_device(): lax.all_gather(keymat, ('dp', 'fsdp'), axis=1, tiled=True)  50.5 us
  transfers between devices with their start and end apart: 17, of which 14 were waited for; matrix products, arithmetic and copies ran while one was open for 14% of the time, Pallas kernels for 0%

profile of v1, /device:TPU:0, one launch (start us, length us, event | category | flops | bytes accessed | tf_op | source)
XLA Modules:
  0.0 1210.0 jit_solution(15888384189764160991)
XLA Ops:
  18.8 42.7 %all-reduce.19 = (bf16[768]{0:T(1024)(128)(2,1)S(1)}, bf16[768]{0:T(1024)(128)(2,1)S(1)}, bf16[768]{0:T(1024)(128)(2,1)S(1)}, bf16[768]{0:T(1024)(128)(2,1)S(1)}...) all-reduce(bf16[768]{0:T(1024)(128)(2,1)S(1)} %dynamic-update-slice, ...), channel_id=1, replica_groups=mesh['dp'=8,'fsdp'=4] {'dp','fsdp'}, use_global_device_ids=true, to_apply=%add.2 | all-reduce | flops 9216 | bytes 36864
  68.0 2.9 add_convert_fusion.2
  73.6 50.5 %all-gather.11.cloned.1.call-done = bf16[768,768]{0,1:T(8,128)(2,1)} async-done(((bf16[768,24]{0,1:T(8,128)(2,1)}), bf16[768,768]{0,1:T(8,128)(2,1)}) %all-gather.11.cloned.1.call-update) | async-done | bytes 1179664 | tf_op jit(solution)/shard_map/all_gather | solution.py:94
  127.0 3.9 reshape.173
  130.9 49.1 %all-gather.7.cloned.1.call-done = bf16[768,768]{0,1:T(8,128)(2,1)} async-done(((bf16[768,24]{0,1:T(8,128)(2,1)}), bf16[768,768]{0,1:T(8,128)(2,1)}) %all-gather.7.cloned.1.call-update) | async-done | bytes 1179664 | tf_op jit(solution)/shard_map/all_gather | solution.py:95
  180.1 2.9 add_convert_fusion.3
  183.0 3.9 reshape.171
  186.9 4.8 fusion.7
  196.1 3.6 convolution_convert_fusion
  199.8 36.1 %all-gather.13.cloned.1.call-done = bf16[768,768]{0,1:T(8,128)(2,1)} async-done(((bf16[768,24]{0,1:T(8,128)(2,1)}), bf16[768,768]{0,1:T(8,128)(2,1)}) %all-gather.13.cloned.1.call-update) | async-done | bytes 1179664 | tf_op jit(solution)/shard_map/all_gather | solution.py:97
  235.9 5.0 fusion.84
  243.0 58.2 %all-gather.15.cloned.1.call-done = bf16[768,3072]{0,1:T(8,128)(2,1)} async-done(((bf16[768,96]{0,1:T(8,128)(2,1)}), bf16[768,3072]{0,1:T(8,128)(2,1)}) %all-gather.15.cloned.1.call-update) | async-done | bytes 4718608 | tf_op jit(solution)/shard_map/all_gather | solution.py:101
  301.2 10.9 fusion.24
  312.1 54.3 %all-gather.17.cloned.1.call-done = bf16[3072,768]{0,1:T(8,128)(2,1)} async-done(((bf16[3072,24]{0,1:T(8,128)(2,1)}), bf16[3072,768]{0,1:T(8,128)(2,1)}) %all-gather.17.cloned.1.call-update) | async-done | bytes 4718608 | tf_op jit(solution)/shard_map/all_gather | solution.py:164
  366.4 16.4 %convert_reduce_fusion = (f32[3072]{0:T(1024)S(1)}, bf16[16,64,3072]{2,1,0:T(8,128)(2,1)S(1)}) fusion(f32[16,64,3072]{2,1,0:T(8,128)} %fusion.24, f32[3072]{0:T(1024)S(1)} %convert_element_type.143, bf16[3072,768]{0,1:T(8,128)(2,1)} %all-gather.17.cloned.1.call-done, bf16[16,64,768]{2,1,0:T(8,128)(2,1)S(1)} %copy-done.11, f32[16,64]{1,0:T(8,128)S(1)} %get-tuple-element.47), kind=kOutput, calls=%fused_computation.9 | convolution fusion | flops 4906546176 | bytes 25194496 | tf_op jit(solution)/shard_map/clj,ij->cli/dot_general | solution.py:44
  382.8 5.5 multiply_reduce_fusion.1
  395.1 6.0 reshape.174
  401.1 9.1 multiply_reduce_fusion
  410.2 3.0 multiply_convert_fusion.3
  415.0 4.6 copy.82
  419.6 6.2 reshape.176
  425.8 4.6 convolution_bitcast_fusion.4
  430.5 5.0 convert_reduce_fusion.2
  435.5 4.7 copy.78
  440.2 6.3 reshape.175
  446.4 4.7 convolution_bitcast_fusion.5
  451.2 6.5 convolution_bitcast_fusion.2
  457.7 6.7 convert_reduce_fusion.1
  464.4 4.6 copy.84
  469.0 5.4 reshape.177
  474.4 3.1 convolution_bitcast_fusion.3
  477.6 11.1 convolution_bitcast_fusion.1
  488.8 12.2 %convolution_bitcast_fusion = f32[3072,768]{0,1:T(8,128)} fusion(bf16[16,64,768]{2,1,0:T(8,128)(2,1)} %param.20, f32[16,64]{1,0:T(8,128)S(1)} %get-tuple-element.47, f32[16,64,3072]{2,1,0:T(8,128)} %fusion.24, f32[3072]{0:T(1024)S(1)} %convert_element_type.143), kind=kOutput, calls=%fused_computation.20 | convolution fusion | flops 4865654784 | bytes 23609344 | tf_op jit(solution)/shard_map/cli,clj->ij/dot_general | solution.py:48
  506.2 7.7 collective-permute-done.1
  517.5 13.6 %collective-permute-done.2 = bf16[3072,96]{0,1:T(8,128)(2,1)} collective-permute-done((bf16[3072,96]{0,1:T(8,128)(2,1)}, bf16[3072,96]{0,1:T(8,128)(2,1)}, u32[]{:S(2)}, u32[]{:S(2)}) %collective-permute-start.2) | collective-permute-done | bytes 589856 | tf_op jit(solution)/shard_map/ppermute | solution.py:15
  531.0 3.1 maximum_select_fusion.2
  536.0 25.0 %collective-permute-done.3 = bf16[3072,192]{0,1:T(8,128)(2,1)} collective-permute-done((bf16[3072,192]{0,1:T(8,128)(2,1)}, bf16[3072,192]{0,1:T(8,128)(2,1)}, u32[]{:S(2)}, u32[]{:S(2)}) %collective-permute-start.3) | collective-permute-done | bytes 1179680 | tf_op jit(solution)/shard_map/ppermute | solution.py:15
  560.9 3.7 maximum_select_fusion.1
  567.0 3.1 fusion.57
  570.1 3.1 fusion.60
  573.3 5.0 fusion.81
  581.7 113.2 %all-reduce.18 = (f32[768]{0:T(1024)S(1)}, f32[768]{0:T(1024)S(1)}, f32[768]{0:T(1024)S(1)}, f32[768]{0:T(1024)S(1)}, f32[768]{0:T(1024)S(1)}, /*index=5*/f32[76...) all-reduce(f32[768]{0:T(1024)S(1)} %get-tuple-element.19, ...), channel_id=2, replica_groups=mesh['dp'=8,'fsdp'=4] {'dp','fsdp'}, use_global_device_ids=true, to_apply=%region_12.13.clone | all-reduce | flops 9216 | bytes 73728
  700.1 4.9 add_add_fusion.2
  705.0 13.5 %add_convert_fusion = bf16[16,64,768]{2,1,0:T(8,128)(2,1)} fusion(f32[16,64,768]{2,1,0:T(8,128)S(1)} %copy-done.9, bf16[3072,384]{0,1:T(8,128)(2,1)} %collective-permute-done.4, bf16[3072,384]{0,1:T(8,128)(2,1)} %maximum_select_fusion.1, pred[]{:T(512)S(6)} %eq.15, f32[768]{0:T(1024)S(1)} %convert_element_type.145, f32[16,64,3072]{2,1,0:T(8,128)} %fusion.24, ...), kind=kOutput, calls=%fused_computation.68 | convolution fusion | flops 4886888448 | bytes 22035456 | tf_op jit(solution)/shard_map/cli,ij->clj/dot_general | solution.py:40
  718.6 96.6 %reduce-scatter.13.cloned.1.call-done = f32[768,24]{0,1:T(8,128)} async-done(((f32[768,768]{0,1:T(8,128)}), f32[768,24]{0,1:T(8,128)}) %reduce-scatter.13.cloned.1.call-update) | async-done | bytes 73744 | tf_op jit(solution)/shard_map/reduce_scatter | solution.py:274
  815.2 104.6 %reduce-scatter.11.cloned.1.call-done = f32[768,24]{0,1:T(8,128)} async-done(((f32[768,768]{0,1:T(8,128)}), f32[768,24]{0,1:T(8,128)}) %reduce-scatter.11.cloned.1.call-update) | async-done | bytes 73744 | tf_op jit(solution)/shard_map/reduce_scatter | solution.py:272
  919.8 141.0 %reduce-scatter.15.cloned.1.call-done = f32[768,96]{0,1:T(8,128)} async-done(((f32[768,3072]{0,1:T(8,128)}), f32[768,96]{0,1:T(8,128)}) %reduce-scatter.15.cloned.1.call-update) | async-done | bytes 294928 | tf_op jit(solution)/shard_map/reduce_scatter | solution.py:204
  1060.8 142.0 %reduce-scatter.17.cloned.1.call-done = f32[3072,24]{0,1:T(8,128)} async-done(((f32[3072,768]{0,1:T(8,128)}), f32[3072,24]{0,1:T(8,128)}) %reduce-scatter.17.cloned.1.call-update) | async-done | bytes 294928 | tf_op jit(solution)/shard_map/reduce_scatter | solution.py:206
  (150 shorter events, 60.4 us)
Async XLA Ops:
  7.2 56.8 %copy-start.1 = (bf16[16,64,768]{2,1,0:T(8,128)(2,1)S(1)}, bf16[16,64,768]{2,1,0:T(8,128)(2,1)}, u32[]{:S(2)}) copy-start(bf16[16,64,768]{2,1,0:T(8,128)(2,1)} %param.18) | copy-start | bytes 4718596
  7.2 60.8 %all-gather.9.cloned.1.call-start = ((), (), s32[]{:S(2)}) async-start(), calls=%async_computation.7 | async-start | bytes 1216512 | tf_op jit(solution)/shard_map/all_gather | solution.py:92
  7.9 116.2 %all-gather.11.cloned.1.call-start = ((), (), s32[]{:S(2)}) async-start(), calls=%async_computation.8 | async-start | bytes 1216512 | tf_op jit(solution)/shard_map/all_gather | solution.py:94
  8.7 171.4 %all-gather.7.cloned.1.call-start = ((), (), s32[]{:S(2)}) async-start(), calls=%async_computation.6 | async-start | bytes 1216512 | tf_op jit(solution)/shard_map/all_gather | solution.py:95
  9.4 226.5 %all-gather.13.cloned.1.call-start = ((), (), s32[]{:S(2)}) async-start(), calls=%async_computation.9 | async-start | bytes 1216512 | tf_op jit(solution)/shard_map/all_gather | solution.py:97
  10.0 291.2 %all-gather.15.cloned.1.call-start = ((), (), s32[]{:S(2)}) async-start(), calls=%async_computation.10 | async-start | bytes 4866048 | tf_op jit(solution)/shard_map/all_gather | solution.py:101
  10.6 355.8 %all-gather.17.cloned.1.call-start = ((), (), s32[]{:S(2)}) async-start(), calls=%async_computation.11 | async-start | bytes 4866048 | tf_op jit(solution)/shard_map/all_gather | solution.py:164
  11.2 707.4 %reduce-scatter.9.cloned.1.call-start = ((), (), s32[]{:S(2)}) async-start(), calls=%async_computation.13 | async-start | bytes 2433024 | tf_op jit(solution)/shard_map/reduce_scatter | solution.py:271
  64.5 0.6 copy-start.17
  191.7 3.2 copy-start
  191.7 4.5 copy-start.6
  240.9 1.6 copy-start.7
  243.0 123.4 %copy-start.11 = (bf16[16,64,768]{2,1,0:T(8,128)(2,1)S(1)}, bf16[16,64,768]{2,1,0:T(8,128)(2,1)}, u32[]{:S(2)}) copy-start(bf16[16,64,768]{2,1,0:T(8,128)(2,1)} %param.20) | copy-start | bytes 4718596
  366.4 16.4 %copy-start.8 = (f32[16,64,768]{2,1,0:T(8,128)S(1)}, f32[16,64,768]{2,1,0:T(8,128)}, u32[]{:S(2)}) copy-start(f32[16,64,768]{2,1,0:T(8,128)} %copy-done.7) | copy-start | bytes 9437188
  366.4 16.4 %copy-start.20 = (bf16[768,3072]{0,1:T(8,128)(2,1)S(1)}, bf16[768,3072]{0,1:T(8,128)(2,1)}, u32[]{:S(2)}) copy-start(bf16[768,3072]{0,1:T(8,128)(2,1)} %all-gather.15.cloned.1.call-done) | copy-start | bytes 14155780
  382.8 5.6 copy-start.24
  389.7 1.7 copy-start.3
  389.7 2.9 copy-start.23
  391.4 1.1 copy-start.15
  395.1 15.1 %slice-start = ((s8[6291456]{0:T(1024)(128)(4,1)}), s8[2097152]{0:T(1024)(128)(4,1)S(1)}, s32[]{:S(2)}) async-start(s8[6291456]{0:T(1024)(128)(4,1)} %bitcast.81), calls=%async_computation.18 | async-start | bytes 4194304
  401.1 9.1 slice-start.1
  410.2 3.0 copy-start.4
  413.2 1.8 copy-start.10
  419.6 6.2 copy-start.2
  430.4 288.1 %reduce-scatter.7.cloned.1.call-start = ((), (), s32[]{:S(2)}) async-start(), calls=%async_computation.12 | async-start | bytes 2433024 | tf_op jit(solution)/shard_map/reduce_scatter | solution.py:269
  451.1 364.1 %reduce-scatter.13.cloned.1.call-start = ((), (), s32[]{:S(2)}) async-start(), calls=%async_computation.15 | async-start | bytes 2433024 | tf_op jit(solution)/shard_map/reduce_scatter | solution.py:274
  457.7 462.1 %reduce-scatter.11.cloned.1.call-start = ((), (), s32[]{:S(2)}) async-start(), calls=%async_computation.14 | async-start | bytes 2433024 | tf_op jit(solution)/shard_map/reduce_scatter | solution.py:272
  477.6 583.2 %reduce-scatter.15.cloned.1.call-start = ((), (), s32[]{:S(2)}) async-start(), calls=%async_computation.16 | async-start | bytes 9732096 | tf_op jit(solution)/shard_map/reduce_scatter | solution.py:204
  488.8 714.0 %reduce-scatter.17.cloned.1.call-start = ((), (), s32[]{:S(2)}) async-start(), calls=%async_computation.17 | async-start | bytes 9732096 | tf_op jit(solution)/shard_map/reduce_scatter | solution.py:206
  501.0 0.9 copy-start.16
  501.9 34.0 %copy-start.19 = (bf16[768]{0:T(1024)(128)(2,1)S(1)}, bf16[768]{0:T(1024)(128)(2,1)}, u32[]{:S(2)}) copy-start(bf16[768]{0:T(1024)(128)(2,1)} %get-tuple-element.38) | copy-start | bytes 4612
  501.9 1.5 collective-permute-start
  504.6 9.3 collective-permute-start.1
  516.0 15.0 %collective-permute-start.2 = (bf16[3072,96]{0,1:T(8,128)(2,1)}, bf16[3072,96]{0,1:T(8,128)(2,1)}, u32[]{:S(2)}, u32[]{:S(2)}) collective-permute-start(bf16[3072,96]{0,1:T(8,128)(2,1)} %maximum_select_fusion.3), channel_id=1, source_target_pairs={{0,4},{1,5},{2,6},{3,7},{4,0},{5,1},{6,2},{7,3},{8,12},{9,13},{10,... | collective-permute-start | bytes 1769480 | tf_op jit(solution)/shard_map/ppermute | solution.py:15
  534.1 26.8 %collective-permute-start.3 = (bf16[3072,192]{0,1:T(8,128)(2,1)}, bf16[3072,192]{0,1:T(8,128)(2,1)}, u32[]{:S(2)}, u32[]{:S(2)}) collective-permute-start(bf16[3072,192]{0,1:T(8,128)(2,1)} %maximum_select_fusion.2), channel_id=1, source_target_pairs={{0,8},{1,9},{2,10},{3,11},{4,12},{5,13},{6,14},{7,15},{8,0},{9,1},... | collective-permute-start | bytes 3538952 | tf_op jit(solution)/shard_map/ppermute | solution.py:15
  535.9 31.1 %copy-start.13 = (bf16[16,64,768]{2,1,0:T(8,128)(2,1)S(1)}, bf16[16,64,768]{2,1,0:T(8,128)(2,1)}, u32[]{:S(2)}) copy-start(bf16[16,64,768]{2,1,0:T(8,128)(2,1)} %reshape.176) | copy-start | bytes 4718596
  536.0 31.1 %copy-start.22 = (bf16[768,768]{0,1:T(8,128)(2,1)S(1)}, bf16[768,768]{0,1:T(8,128)(2,1)}, u32[]{:S(2)}) copy-start(bf16[768,768]{0,1:T(8,128)(2,1)} %all-gather.11.cloned.1.call-done) | copy-start | bytes 3538948
  564.6 5.4 copy-start.14
  564.6 5.4 copy-start.21
  564.6 140.4 %collective-permute-start.4 = (bf16[3072,384]{0,1:T(8,128)(2,1)}, bf16[3072,384]{0,1:T(8,128)(2,1)}, u32[]{:S(2)}, u32[]{:S(2)}) collective-permute-start(bf16[3072,384]{0,1:T(8,128)(2,1)} %maximum_select_fusion.1), channel_id=1, source_target_pairs={{0,16},{1,17},{2,18},{3,19},{4,20},{5,21},{6,22},{7,23},{8,24},{9,... | collective-permute-start | bytes 7077896 | tf_op jit(solution)/shard_map/ppermute | solution.py:15
  573.3 5.1 copy-start.18
  578.3 1.7 copy-start.5
  578.3 121.8 %copy-start.12 = (bf16[16,64,768]{2,1,0:T(8,128)(2,1)S(1)}, bf16[16,64,768]{2,1,0:T(8,128)(2,1)}, u32[]{:S(2)}) copy-start(bf16[16,64,768]{2,1,0:T(8,128)(2,1)} %param.20) | copy-start | bytes 4718596
  700.1 4.9 copy-start.9
Sparse Core Ops, SparseCore 0:
  10.9 56.9 all-gather.8
  70.9 53.1 all-gather.10
  127.0 53.0 all-gather.6
  182.8 53.0 all-gather.12
  238.6 62.5 all-gather.14
  304.0 62.3 all-gather.16
  430.6 97.7 reduce-scatter.8
  535.1 176.1 reduce-scatter.6
  717.2 97.9 reduce-scatter.12
  821.7 97.9 reduce-scatter.10
  926.2 134.4 reduce-scatter.14
  1068.1 134.5 reduce-scatter.16
